TPU v7x, 512 devices: a whole 4x4x16 slice. The times are simulated.
512 devices in a mesh: vox: 64 (over z, x_hi, core), tm: 4 (over y), mod: 2 (over x_lo).
Axes of the slice: x: 4 (x_hi: 2, x_lo: 2; x = x_hi * 2 + x_lo), y: 4, z: 16, core: 2. Of those that a mesh axis runs over, the one named last changes fastest.
Arguments:
- scans: bfloat16 [2, 16384, 48, 512], P('mod', 'vox', None, 'tm'), may hold values from -6 to 6
- spatial_init: float32 [2, 16384, 128], P('mod', 'vox'), may hold values from -6 to 6
- time_init: float32 [512, 128], P('tm'), may hold values from -0.09375 to 0.09375
- subject_init: float32 [48, 128], replicated, may hold values from -6 to 6
- hrf_kernel: float32 [16], replicated, may hold values from 0.05 to 0.5
- kept_blocks: int32 [48, 32], P(None, 'tm'), may hold values 0 or 1
Outputs:
- spatial_factors: float32 [2, 16384, 128], P('mod', 'vox')
- time_factors: float32 [512, 128], P('tm')
- subject_factors: float32 [48, 128], replicated
All inputs are finite; a program needn't handle non-finite values. No bound on the sum of `kept_blocks` on one device may be relied on, other than what follows from the above.
Results may differ from a plain program's by a relative error of at most 0.003.
Values sent between devices are 32-bit elements; how exact they have to be, the bound alone decides.
A program may use at most 64 MiB of HBM per device.

v0:
```python
import jax
import jax.numpy as jnp
from jax import lax
from jax.sharding import PartitionSpec as P

RIDGE = 0.1
EPS = 1e-06


def shifted(block, axis, distance):
    devices = range(lax.axis_size(axis))
    route = [(i - distance, i) for i in devices if i - distance in devices]
    return lax.ppermute(block, axis, route)


def ridge_solve(right_side, gram):
    eye_mat = jnp.eye(gram.shape[0], dtype=gram.dtype)
    factor = jnp.linalg.cholesky(gram + RIDGE * eye_mat)
    return jax.scipy.linalg.cho_solve((factor, True), right_side.T).T


def hgram(left, right):
    return jnp.dot(left.T, right, precision=lax.Precision.HIGHEST)


def conv_causal(series, kernel):
    reach = kernel.shape[0]
    count = series.shape[0]
    tail_part = series[count - (reach - 1) :]
    before = shifted(tail_part, "tm", 1)
    padded = jnp.concatenate([before, series])
    summed = jnp.zeros_like(series)
    for lag in range(reach):
        summed = summed + kernel[lag] * padded[reach - 1 - lag : reach - 1 - lag + count]
    return summed


def conv_adjoint(series, kernel):
    reach = kernel.shape[0]
    count = series.shape[0]
    head_part = series[: reach - 1]
    after = shifted(head_part, "tm", -1)
    padded = jnp.concatenate([series, after])
    summed = jnp.zeros_like(series)
    for lag in range(reach):
        summed = summed + kernel[lag] * padded[lag : lag + count]
    return summed


def per_device(scans, spatial_init, time_init, subject_init, hrf_kernel, kept_blocks):
    is_fmri = lax.axis_index("mod") == 0
    row_count, subj_count, tr_count = (scans.shape[1], scans.shape[2], scans.shape[3])
    rank_count = subject_init.shape[1]
    total_rows = row_count * lax.axis_size("vox")
    total_trs = tr_count * lax.axis_size("tm")
    factor_t = jnp.where(is_fmri, conv_causal(time_init, hrf_kernel), time_init)
    block_len = tr_count // kept_blocks.shape[1]
    kept_tr = jnp.logical_or(
        jnp.repeat(kept_blocks, block_len, axis=1) > 0, jnp.logical_not(is_fmri)
    )
    khatri = (
        (subject_init[:, None, :] * factor_t[None, :, :])
        .astype(jnp.bfloat16)
        .reshape(subj_count * tr_count, rank_count)
    )
    signal = scans[0].reshape(row_count, subj_count * tr_count)
    previous = spatial_init[0].astype(jnp.bfloat16)
    modeled = lax.dot_general(
        previous, khatri, (((1,), (1,)), ((), ())), preferred_element_type=jnp.float32
    )
    filled = jnp.where(
        kept_tr.reshape(1, subj_count * tr_count), signal.astype(jnp.float32), modeled
    ).astype(jnp.bfloat16)
    mttkrp_part = jnp.dot(filled, khatri, preferred_element_type=jnp.float32)
    tgram_part = hgram(factor_t, factor_t)
    mttkrp, time_gram = lax.psum((mttkrp_part, tgram_part), "tm")
    subj_gram = hgram(subject_init, subject_init)
    updated = ridge_solve(mttkrp, subj_gram * time_gram)
    rgram_part = hgram(updated, updated)
    khatri2 = (
        (updated[:, None, :] * subject_init[None, :, :])
        .astype(jnp.bfloat16)
        .reshape(row_count * subj_count, rank_count)
    )
    proj = lax.dot_general(
        filled.reshape(row_count * subj_count, tr_count),
        khatri2,
        (((0,), (0,)), ((), ())),
        preferred_element_type=jnp.float32,
    )
    adjoint = jnp.where(is_fmri, conv_adjoint(proj, hrf_kernel), proj)
    tgram_terms = rgram_part * subj_gram
    time_rhs, gram_t = lax.psum((adjoint, tgram_terms), ("vox", "mod"))
    raw = total_rows * ridge_solve(time_rhs, gram_t)
    sumsq = lax.psum(jnp.sum(raw * raw, axis=0), "tm")
    time_factors = raw / jnp.sqrt(sumsq / total_trs + EPS)
    scale_c = (2.0 * total_rows * total_trs) ** (-0.5)
    scaled_eeg = time_factors * scale_c
    scaled_t = jnp.where(is_fmri, conv_causal(scaled_eeg, hrf_kernel), scaled_eeg)
    khatri3 = (updated[:, None, :] * scaled_t[None, :, :]).astype(jnp.bfloat16)
    subj_part = lax.dot_general(
        filled.reshape(row_count, subj_count, tr_count),
        khatri3,
        (((0, 2), (0, 1)), ((), ())),
        preferred_element_type=jnp.float32,
    )
    sgram_part = hgram(scaled_t, scaled_t)
    row_gram = lax.psum(rgram_part, "vox")
    scaled_gram = lax.psum(sgram_part, "tm")
    leading = jnp.logical_and(lax.axis_index("vox") == 0, lax.axis_index("tm") == 0)
    gram_term = jnp.where(leading, row_gram * scaled_gram, 0.0)
    subject_rhs, gram_c = lax.psum((subj_part, gram_term), ("vox", "tm", "mod"))
    subject_factors = ridge_solve(subject_rhs, gram_c)
    return (updated[None], time_factors, subject_factors)


def solution(mesh):
    return jax.shard_map(
        per_device,
        mesh=mesh,
        in_specs=(
            P("mod", "vox", None, "tm"),
            P("mod", "vox", None),
            P("tm", None),
            P(),
            P(),
            P(None, "tm"),
        ),
        out_specs=(P("mod", "vox", None), P("tm", None), P()),
        check_vma=False,
    )
```

profile of v0, /device:TPU:1, one launch (start us, length us, event | category | flops | bytes accessed | tf_op | source)
XLA Modules:
  0.0 1485.5 jit_solution(1407539403140570844)
XLA Ops:
  7.9 4.0 collective-permute-start
  12.6 1.9 fusion.160
  14.6 5.1 copy.23
  20.1 10.2 fusion.98
  31.6 4.8 fusion.4
  36.4 1.7 fusion.163
  38.4 3.1 copy.26
  41.5 5.7 reshape.87
  47.2 50.4 %all-reduce.16.cloned.1.call-done = (f32[256,128]{1,0:T(8,128)}, f32[128,128]{1,0:T(8,128)}) async-done(((f32[256,128]{1,0:T(8,128)}, f32[128,128]{1,0:T(8,128)}), (f32[256,128]{1,0:T(8,128)}, f32[128,128]{1,0:T(8,128)})) %all-reduce.16.cloned.1.call-update) | async-done | bytes 196624 | tf_op jit(solution)/shard_map/psum | solution.py:76
  99.0 11.7 cholesky.59
  112.0 9.8 custom-call.23
  121.9 1.2 fusion.156
  124.0 1.3 copy-done
  126.4 1.3 collective-permute-start.1
  128.6 2.2 collective-permute-done.1
  130.8 10.8 fusion.54
  141.9 322.2 %all-reduce.14.cloned.1.call-done = (f32[128,128]{1,0:T(8,128)}, f32[128,128]{1,0:T(8,128)}) async-done(((f32[128,128]{1,0:T(8,128)}, f32[128,128]{1,0:T(8,128)}), (f32[128,128]{1,0:T(8,128)}, f32[128,128]{1,0:T(8,128)})) %all-reduce.14.cloned.1.call-update) | async-done | bytes 131088 | tf_op jit(solution)/shard_map/psum | solution.py:93
  466.6 12.5 cholesky.70
  479.8 1.3 fusion.139
  481.1 10.6 custom-call.24
  493.2 8.5 psum.67
  502.3 1.3 collective-permute-start.2
  504.4 10.4 fusion.10
  515.7 3.5 copy.32
  519.9 429.4 %all-reduce.8.cloned.1.call-done = f32[128,128]{1,0:T(8,128)} async-done(((f32[128,128]{1,0:T(8,128)}), f32[128,128]{1,0:T(8,128)}) %all-reduce.8.cloned.1.call-update) | async-done | bytes 65552 | tf_op jit(solution)/shard_map/psum | solution.py:108
  949.3 54.3 %all-reduce.10.cloned.1.call-done = f32[128,128]{1,0:T(8,128)} async-done(((f32[128,128]{1,0:T(8,128)}), f32[128,128]{1,0:T(8,128)}) %all-reduce.10.cloned.1.call-update) | async-done | bytes 65552 | tf_op jit(solution)/shard_map/psum | solution.py:109
  1003.6 1.5 multiply_select_fusion
  1005.2 3.2 fusion.5
  1008.4 106.8 %psum.71 = f32[48,128]{1,0:T(8,128)S(1)} all-reduce(f32[48,128]{1,0:T(8,128)S(1)} %fusion.5), channel_id=1, replica_groups=mesh['vox'=64,'tm'=4,'mod'=2] {'vox','tm','mod'}, use_global_device_ids=true, to_apply=%region_11.13 | all-reduce | flops 6144 | bytes 49152 | tf_op jit(solution)/shard_map/psum | solution.py:112
  1115.1 337.9 %all-reduce.12.cloned.1.call-done = f32[128,128]{1,0:T(8,128)} async-done(((f32[128,128]{1,0:T(8,128)}), f32[128,128]{1,0:T(8,128)}) %all-reduce.12.cloned.1.call-update) | async-done | bytes 65552 | tf_op jit(solution)/shard_map/psum | solution.py:112
  1455.0 11.7 cholesky.81
  1468.0 9.8 custom-call.25
  (61 shorter events, 20.7 us)
Async XLA Ops:
  7.2 90.5 %all-reduce.16.cloned.1.call-start = ((), (), s32[]{:S(2)}) async-start(), calls=%async_computation.4 | async-start | bytes 393216 | tf_op jit(solution)/shard_map/psum | solution.py:76
  7.9 12.2 collective-permute-start
  14.6 5.5 copy-start.3
  14.6 16.6 %copy-start.1 = (f32[48,128]{1,0:T(8,128)S(1)}, f32[48,128]{1,0:T(8,128)}, u32[]{:S(2)}) copy-start(f32[48,128]{1,0:T(8,128)} %param.10) | copy-start | bytes 73732
  14.6 17.0 %copy-start.2 = (f32[1,256,128]{2,1,0:T(8,128)S(1)}, f32[1,256,128]{2,1,0:T(8,128)}, u32[]{:S(2)}) copy-start(f32[1,256,128]{2,1,0:T(8,128)} %param.8) | copy-start | bytes 393220
  38.1 425.9 %all-reduce.14.cloned.1.call-start = ((), (), s32[]{:S(2)}) async-start(), calls=%async_computation.3 | async-start | bytes 262144 | tf_op jit(solution)/shard_map/psum | solution.py:93
  123.4 1.9 copy-start
  126.4 4.4 collective-permute-start.1
  141.6 807.7 %all-reduce.8.cloned.1.call-start = ((), (), s32[]{:S(2)}) async-start(), calls=%async_computation | async-start | bytes 131072 | tf_op jit(solution)/shard_map/psum | solution.py:108
  502.3 2.1 collective-permute-start.2
  504.3 499.4 %all-reduce.10.cloned.1.call-start = ((), (), s32[]{:S(2)}) async-start(), calls=%async_computation.1 | async-start | bytes 131072 | tf_op jit(solution)/shard_map/psum | solution.py:109
  515.7 937.4 %all-reduce.12.cloned.1.call-start = ((), (), s32[]{:S(2)}) async-start(), calls=%async_computation.2 | async-start | bytes 131072 | tf_op jit(solution)/shard_map/psum | solution.py:112
Sparse Core Ops, SparseCore 0:
  38.3 59.3 all-reduce.15
  141.7 322.2 all-reduce.13
  504.4 444.8 all-reduce.7
  951.5 52.1 all-reduce.9
  1009.8 443.1 all-reduce.11
where the time goes:
time: 1490 us
  waiting for transfers between devices  1200 us (81%)
  blocking collectives  115 us (8%)
  other arithmetic  109 us (7%)
  local copies, waits for them, and re-layouts  23.8 us (2%)
  matrix products  18.6 us (1%)
    psum x1, waiting for transfers between devices, per_device(): row_gram = lax.psum(rgram_part, 'vox')  429 us
    psum x1, waiting for transfers between devices, per_device(): subject_rhs, gram_c = lax.psum((subj_part, gram_term), ('vox', 'tm', 'mod'))  338 us
    psum x1, waiting for transfers between devices, per_device(): time_rhs, gram_t = lax.psum((adjoint, tgram_terms), ('vox', 'mod'))  322 us
    psum x1, blocking collectives, per_device(): subject_rhs, gram_c = lax.psum((subj_part, gram_term), ('vox', 'tm', 'mod'))  107 us
    psum x1, waiting for transfers between devices, per_device(): scaled_gram = lax.psum(sgram_part, 'tm')  54.3 us
    psum x1, waiting for transfers between devices, per_device(): mttkrp, time_gram = lax.psum((mttkrp_part, tgram_part), 'tm')  50.4 us
    another operation x9, other arithmetic, ridge_solve(): factor = jnp.linalg.cholesky(gram + RIDGE * eye_mat)  38 us
    another operation x6, other arithmetic, ridge_solve(): return jax.scipy.linalg.cho_solve((factor, True), right_side.T).T  32.9 us
  transfers between devices with their start and end apart: 8, of which 7 were waited for; matrix products, arithmetic and copies ran while one was open for 2% of the time, Pallas kernels for 0%

commit v1 on v0

v1 whole, which is shorter than its diff:
```python
import functools

import jax
import jax.numpy as jnp
from jax import lax
from jax.experimental import pallas as pl
from jax.experimental.pallas import tpu as pltpu
from jax.sharding import PartitionSpec as P

RIDGE = 0.1
EPS = 1e-06
MESH = pl.DeviceIdType.MESH
PLANE = 4
HIGHEST = lax.Precision.HIGHEST


def dot(a, b):
    return jnp.dot(a, b, precision=HIGHEST, preferred_element_type=jnp.float32)


def tdot(a, b):
    return lax.dot_general(
        a, b, (((0,), (0,)), ((), ())), precision=HIGHEST, preferred_element_type=jnp.float32
    )


def spd_inverse(gram):
    n = gram.shape[0]
    lane = lax.broadcasted_iota(jnp.int32, (8, n), 1)
    sub = lax.broadcasted_iota(jnp.int32, (8, n), 0)
    eye8 = jnp.where(lane == sub, 1.0, 0.0)
    inside = lane < 8
    ridge = jnp.where(
        lax.broadcasted_iota(jnp.int32, (n, n), 0) == lax.broadcasted_iota(jnp.int32, (n, n), 1),
        RIDGE,
        0.0,
    )

    def step(_, mat):
        top = mat[0:8]
        cols = [jnp.broadcast_to(top[:, j : j + 1], (8, n)) for j in range(8)]
        row = jnp.where(inside, eye8, top)
        for i in range(8):
            gain = jnp.where(sub == i, -1.0, cols[i]) * (1.0 / cols[i][i : i + 1])
            row = jnp.where(sub == i, 0.0, row) - gain * row[i : i + 1]
            for j in range(i + 1, 8):
                cols[j] = jnp.where(sub == i, 0.0, cols[j]) - gain * cols[j][i : i + 1]
        rows = []
        for b in range(1, n // 8):
            below = mat[8 * b : 8 * b + 8]
            left = jnp.where(inside, 0.0, below)
            for j in range(8):
                left = left - jnp.broadcast_to(below[:, j : j + 1], (8, n)) * row[j : j + 1]
            rows.append(left)
        return pltpu.roll(jnp.concatenate(rows + [row]), n - 8, 1)

    return lax.fori_loop(0, n // 8, step, gram + ridge, unroll=2)


def sweep(
    sizes,
    scans,
    spatial,
    time_init,
    subject,
    hrf,
    kept,
    out_spatial,
    out_time,
    out_subject,
    x_in,
    x_f32,
    xs,
    mask,
    pad,
    factors,
    rhs,
    rhs_in,
    updated,
    gram_part,
    g1,
    g2,
    g_sum,
    g_all,
    ppad,
    ext,
    halo,
    r1,
    r2,
    r_sum,
    r_all,
    s_part,
    s1,
    s2,
    s_sum,
    s_own,
    s_all,
    local_sem,
    send_sem,
    recv_sem,
    halo_sem,
):
    nz, ntm, nmod = sizes
    rows, rank = spatial.shape
    subjects = subject.shape[0]
    trs = time_init.shape[0]
    reach = hrf.shape[0]
    vox, tm, mod = lax.axis_index("vox"), lax.axis_index("tm"), lax.axis_index("mod")
    z, c4 = vox // PLANE, vox % PLANE
    nplane = PLANE * ntm * nmod
    place = (c4 * ntm + tm) * nmod + mod
    ngram = PLANE * ntm
    gplace = c4 * ntm + tm
    nrhs = PLANE * nmod
    rplace = c4 * nmod + mod
    grow = rank // ngram
    rrow = trs // nrhs
    srow = subjects // nz
    own = pl.ds(pl.multiple_of(trs * tm, trs), trs)
    part = rows // ntm
    my_part = pl.ds(pl.multiple_of(part * tm, part), part)

    def along_tm(d):
        return (vox, lax.rem(tm + d, ntm), mod)

    def along_z(d):
        return (lax.rem(z + d, nz) * PLANE + c4, tm, mod)

    def in_plane(d):
        to = lax.rem(place + d, nplane)
        return (z * PLANE + to // (ntm * nmod), lax.rem(to // nmod, ntm), lax.rem(to, nmod))

    def send(stage, src, dst, device):
        pltpu.make_async_remote_copy(
            src_ref=src,
            dst_ref=dst,
            send_sem=send_sem.at[stage],
            recv_sem=recv_sem.at[stage],
            device_id=device,
            device_id_type=MESH,
        ).start()

    def every(count, body):
        def step(d, carry):
            body(d)
            return carry

        lax.fori_loop(1, count, step, 0)

    def wait(sem, stage, ref):
        pltpu.make_async_copy(ref, ref, sem.at[stage]).wait()

    load = pltpu.make_async_copy(scans, x_in, local_sem)
    load.start()
    barrier = pltpu.get_barrier_semaphore()
    every(
        nplane,
        lambda d: pl.semaphore_signal(barrier, 1, device_id=in_plane(d), device_id_type=MESH),
    )
    every(
        nz, lambda d: pl.semaphore_signal(barrier, 1, device_id=along_z(d), device_id_type=MESH)
    )
    pl.semaphore_wait(barrier, nplane + nz - 2)

    pad[0:reach] = jnp.zeros((reach, rank), jnp.float32)
    own_pad = pl.ds(pl.multiple_of(reach + trs * tm, 8), trs)
    every(ntm, lambda d: send(0, time_init, pad.at[own_pad], along_tm(d)))

    load.wait()

    def widen(i, carry):
        at = pl.ds(pl.multiple_of(i * 512, 512), 512)
        x_f32[at] = x_in[at].astype(jnp.float32)
        return carry

    lax.fori_loop(0, rows * subjects // 512, widen, 0)

    def regroup(s, carry):
        xs[pl.ds(pl.multiple_of(s * rows, rows), rows)] = x_f32[
            pl.ds(s, rows, subjects), :
        ].astype(jnp.bfloat16)
        return carry

    lax.fori_loop(0, subjects, regroup, 0)
    block = trs // kept.shape[1]
    block_of = lax.broadcasted_iota(jnp.int32, (subjects, trs), 1) // block
    flags = kept[...]
    keep = jnp.zeros((subjects, trs), jnp.int32)
    for b in range(kept.shape[1]):
        keep = jnp.where(block_of == b, flags[:, b : b + 1], keep)
    mask[...] = jnp.where(mod == 0, keep, 1).astype(jnp.float32)
    subj = subject[...]
    subj_gram = tdot(subj, subj)
    previous = spatial[...].astype(jnp.bfloat16)
    is_fmri = mod == 0
    lags = [hrf[k] for k in range(reach)]
    taps = [jnp.where(is_fmri, lags[k], 1.0 if k == 0 else 0.0) for k in range(reach)]

    pad[own_pad] = time_init[...]
    wait(recv_sem, 0, pad.at[pl.ds(reach, (ntm - 1) * trs)])

    def conv(weights, base):
        summed = weights[0] * pad[reach + base : reach + base + trs]
        for k in range(1, reach):
            summed = summed + weights[k] * pad[reach + base - k : reach + base - k + trs]
        return summed

    for i in range(ntm):
        factors[i * trs : (i + 1) * trs] = conv(taps, i * trs)
    factor = factors[own]
    everything = factors[...]
    time_gram = tdot(everything, everything)

    rhs[...] = jnp.zeros_like(rhs)

    def fill(i, carry):
        s = 2 * i
        first = pl.ds(pl.multiple_of(s * rows, rows), rows)
        second = pl.ds(pl.multiple_of((s + 1) * rows, rows), rows)
        khatri = jnp.concatenate(
            [
                (subject[pl.ds(s, 1)] * factor).astype(jnp.bfloat16),
                (subject[pl.ds(s + 1, 1)] * factor).astype(jnp.bfloat16),
            ]
        )
        modeled = lax.dot_general(
            previous, khatri, (((1,), (1,)), ((), ())), preferred_element_type=jnp.float32
        )
        f0 = jnp.where(
            mask[pl.ds(s, 1)] > 0, xs[first].astype(jnp.float32), modeled[:, :trs]
        ).astype(jnp.bfloat16)
        f1 = jnp.where(
            mask[pl.ds(s + 1, 1)] > 0, xs[second].astype(jnp.float32), modeled[:, trs:]
        ).astype(jnp.bfloat16)
        xs[first] = f0
        xs[second] = f1
        rhs[...] += jnp.dot(
            jnp.concatenate([f0, f1], axis=1), khatri, preferred_element_type=jnp.float32
        )
        return carry

    lax.fori_loop(0, subjects // 2, fill, 0)

    def scatter_rows(d):
        to = pl.multiple_of(part * lax.rem(tm + d, ntm), part)
        send(1, rhs.at[pl.ds(to, part)], rhs_in.at[d - 1], along_tm(d))

    every(ntm, scatter_rows)
    inverse = spd_inverse(subj_gram * time_gram)
    wait(recv_sem, 1, rhs_in)
    mine = rhs[my_part]
    for d in range(ntm - 1):
        mine = mine + rhs_in[d]
    solved = dot(mine, inverse)
    updated[my_part] = solved
    every(ntm, lambda d: send(2, updated.at[my_part], updated.at[my_part], along_tm(d)))

    gram_part[...] = tdot(solved, solved)

    def scatter_gram(d):
        to = lax.rem(gplace + d, ngram)
        send(
            3,
            gram_part.at[pl.ds(pl.multiple_of(grow * to, grow), grow)],
            g1.at[d - 1],
            (z * PLANE + to // ntm, lax.rem(to, ntm), mod),
        )

    every(ngram, scatter_gram)
    wait(recv_sem, 2, updated.at[pl.ds(0, (ntm - 1) * part)])
    upd = updated[...]
    out_spatial[...] = upd

    wait(recv_sem, 3, g1)
    mine = gram_part[pl.ds(pl.multiple_of(grow * gplace, grow), grow)]
    for d in range(ngram - 1):
        mine = mine + g1[d]
    g2[z] = mine
    every(nz, lambda d: send(4, g2.at[z], g2.at[z], along_z(d)))

    def project(i, proj):
        s = 2 * i
        khatri = jnp.concatenate(
            [
                (upd * subject[pl.ds(s, 1)]).astype(jnp.bfloat16),
                (upd * subject[pl.ds(s + 1, 1)]).astype(jnp.bfloat16),
            ]
        )
        filled = xs[pl.ds(pl.multiple_of(s * rows, rows), 2 * rows)]
        return proj + lax.dot_general(
            filled, khatri, (((0,), (0,)), ((), ())), preferred_element_type=jnp.float32
        )

    proj = lax.fori_loop(0, subjects // 2, project, jnp.zeros((trs, rank), jnp.float32))
    ppad[0:reach] = jnp.zeros((reach, rank), jnp.float32)
    ppad[reach : reach + trs] = proj
    ppad[reach + trs :] = jnp.zeros((reach, rank), jnp.float32)
    spread = taps[0] * ppad[0 : reach + trs]
    for k in range(1, reach):
        spread = spread + taps[k] * ppad[k : k + reach + trs]
    ext[...] = spread

    def scatter_time(d):
        to = lax.rem(rplace + d, nrhs)
        send(
            6,
            ext.at[pl.ds(pl.multiple_of(reach + rrow * to, 8), rrow)],
            r1.at[d - 1],
            (z * PLANE + to // nmod, tm, lax.rem(to, nmod)),
        )

    every(nrhs, scatter_time)
    gives_halo = jnp.logical_and(is_fmri, tm > 0)
    takes_halo = jnp.logical_and(rplace == nrhs - 1, tm < ntm - 1)
    halo_copy = pltpu.make_async_remote_copy(
        src_ref=ext.at[pl.ds(0, rrow)],
        dst_ref=halo.at[c4],
        send_sem=halo_sem.at[0],
        recv_sem=halo_sem.at[1],
        device_id=(z * PLANE + PLANE - 1, lax.rem(tm + ntm - 1, ntm), nmod - 1),
        device_id_type=MESH,
    )
    halo_all = pltpu.make_async_copy(halo, halo, halo_sem.at[1])

    @pl.when(gives_halo)
    def _():
        halo_copy.start()

    wait(recv_sem, 4, g2.at[pl.ds(0, nz - 1)])
    mine = g2[0]
    for i in range(1, nz):
        mine = mine + g2[i]
    g_sum[...] = mine
    g_own = mod * ngram + gplace
    g_all[g_own] = mine
    every(nplane, lambda d: send(5, g_sum, g_all.at[g_own], in_plane(d)))

    wait(recv_sem, 6, r1)
    mine = ext[pl.ds(pl.multiple_of(reach + rrow * rplace, 8), rrow)]
    for d in range(nrhs - 1):
        mine = mine + r1[d]
    r2[z] = mine

    @pl.when(takes_halo)
    def _():
        halo_all.wait()
        total = r2[z]
        for i in range(PLANE):
            total = total + halo[i]
        r2[z] = total

    every(nz, lambda d: send(7, r2.at[z], r2.at[z], along_z(d)))

    wait(recv_sem, 5, g_all.at[pl.ds(0, nplane - 1)])
    grams = [
        jnp.concatenate([g_all[m * ngram + i] for i in range(ngram)]) for m in range(nmod)
    ]
    inverse = spd_inverse((grams[0] + grams[1]) * subj_gram)

    wait(recv_sem, 7, r2.at[pl.ds(0, nz - 1)])
    mine = r2[0]
    for i in range(1, nz):
        mine = mine + r2[i]
    r_sum[...] = mine
    r_own = tm * nrhs + rplace
    r_all[r_own] = mine
    every(nplane, lambda d: send(8, r_sum, r_all.at[r_own], in_plane(d)))
    wait(recv_sem, 8, r_all.at[pl.ds(0, nplane - 1)])
    right = jnp.concatenate([r_all[i] for i in range(ntm * nrhs)])
    raw = (rows * nz * PLANE) * dot(right, inverse)
    mean = jnp.sum(raw * raw, axis=0, keepdims=True) / (ntm * trs)
    fresh = raw / jnp.sqrt(mean + EPS)
    scale_c = (2.0 * rows * nz * PLANE * trs * ntm) ** (-0.5)
    pad[reach:] = fresh
    out_time[...] = pad[own_pad]
    pad[reach:] = fresh * scale_c
    for i in range(ntm):
        factors[i * trs : (i + 1) * trs] = conv(lags, i * trs)
    scaled = jnp.where(is_fmri, factors[own], pad[own_pad])
    high = scaled.astype(jnp.bfloat16)
    low = (scaled - high.astype(jnp.float32)).astype(jnp.bfloat16)
    halves = jnp.concatenate([high, low], axis=1)

    def contract(i, carry):
        lines = []
        for j in range(srow):
            s = i * srow + j
            both = jnp.dot(
                xs[pl.ds(pl.multiple_of(s * rows, rows), rows)],
                halves,
                preferred_element_type=jnp.float32,
            )
            lines.append(
                jnp.sum((both[:, :rank] + both[:, rank:]) * upd, axis=0, keepdims=True)
            )
        s_part[i] = jnp.concatenate(lines)
        return carry

    lax.fori_loop(0, nz, contract, 0)
    every(nz, lambda d: send(9, s_part.at[lax.rem(z + d, nz)], s1.at[d - 1], along_z(d)))
    eeg = pad[reach:]
    fmri = factors[...]
    gram_c = grams[0] * tdot(fmri, fmri) + grams[1] * tdot(eeg, eeg)

    wait(recv_sem, 9, s1)
    mine = s_part[z]
    for d in range(nz - 1):
        mine = mine + s1[d]
    s_own[...] = mine
    s2[place] = mine
    every(nplane, lambda d: send(10, s_own, s2.at[place], in_plane(d)))
    inverse = spd_inverse(gram_c)
    wait(recv_sem, 10, s2.at[pl.ds(0, nplane - 1)])
    mine = s2[0]
    for i in range(1, nplane):
        mine = mine + s2[i]
    s_sum[...] = mine
    s_all[z] = mine
    every(nz, lambda d: send(11, s_sum, s_all.at[z], along_z(d)))
    wait(recv_sem, 11, s_all.at[pl.ds(0, nz - 1)])
    out_subject[...] = dot(jnp.concatenate([s_all[i] for i in range(nz)]), inverse)

    wait(send_sem, 0, pad.at[pl.ds(reach, (ntm - 1) * trs)])
    wait(send_sem, 1, rhs_in)
    wait(send_sem, 2, updated.at[pl.ds(0, (ntm - 1) * part)])
    wait(send_sem, 3, g1)
    wait(send_sem, 4, g2.at[pl.ds(0, nz - 1)])
    wait(send_sem, 5, g_all.at[pl.ds(0, nplane - 1)])
    wait(send_sem, 6, r1)
    wait(send_sem, 7, r2.at[pl.ds(0, nz - 1)])
    wait(send_sem, 8, r_all.at[pl.ds(0, nplane - 1)])
    wait(send_sem, 9, s1)
    wait(send_sem, 10, s2.at[pl.ds(0, nplane - 1)])
    wait(send_sem, 11, s_all.at[pl.ds(0, nz - 1)])

    @pl.when(gives_halo)
    def _():
        halo_copy.wait_send()


def per_device(scans, spatial_init, time_init, subject_init, hrf_kernel, kept_blocks):
    nz = lax.axis_size("vox") // PLANE
    ntm, nmod = lax.axis_size("tm"), lax.axis_size("mod")
    _, rows, subjects, trs = scans.shape
    rank = subject_init.shape[1]
    reach = hrf_kernel.shape[0]
    nplane, ngram, nrhs = PLANE * ntm * nmod, PLANE * ntm, PLANE * nmod
    grow, rrow, srow = rank // ngram, trs // nrhs, subjects // nz
    f32, bf16 = jnp.float32, jnp.bfloat16
    vmem = pl.BlockSpec(memory_space=pltpu.VMEM)
    updated, time_factors, subject_factors = pl.pallas_call(
        functools.partial(sweep, (nz, ntm, nmod)),
        out_shape=(
            jax.ShapeDtypeStruct((rows, rank), f32),
            jax.ShapeDtypeStruct((trs, rank), f32),
            jax.ShapeDtypeStruct((subjects, rank), f32),
        ),
        in_specs=[
            pl.BlockSpec(memory_space=pl.ANY),
            vmem,
            vmem,
            vmem,
            pl.BlockSpec(memory_space=pltpu.SMEM),
            vmem,
        ],
        out_specs=(vmem, vmem, vmem),
        scratch_shapes=[
            pltpu.VMEM((rows * subjects, trs), bf16),
            pltpu.VMEM((rows * subjects, trs), f32),
            pltpu.VMEM((subjects * rows, trs), bf16),
            pltpu.VMEM((subjects, trs), f32),
            pltpu.VMEM((reach + ntm * trs, rank), f32),
            pltpu.VMEM((ntm * trs, rank), f32),
            pltpu.VMEM((rows, rank), f32),
            pltpu.VMEM((ntm - 1, rows // ntm, rank), f32),
            pltpu.VMEM((rows, rank), f32),
            pltpu.VMEM((rank, rank), f32),
            pltpu.VMEM((ngram - 1, grow, rank), f32),
            pltpu.VMEM((nz, grow, rank), f32),
            pltpu.VMEM((grow, rank), f32),
            pltpu.VMEM((nplane, grow, rank), f32),
            pltpu.VMEM((2 * reach + trs, rank), f32),
            pltpu.VMEM((reach + trs, rank), f32),
            pltpu.VMEM((PLANE, rrow, rank), f32),
            pltpu.VMEM((nrhs - 1, rrow, rank), f32),
            pltpu.VMEM((nz, rrow, rank), f32),
            pltpu.VMEM((rrow, rank), f32),
            pltpu.VMEM((nplane, rrow, rank), f32),
            pltpu.VMEM((nz, srow, rank), f32),
            pltpu.VMEM((nz - 1, srow, rank), f32),
            pltpu.VMEM((nplane, srow, rank), f32),
            pltpu.VMEM((srow, rank), f32),
            pltpu.VMEM((srow, rank), f32),
            pltpu.VMEM((nz, srow, rank), f32),
            pltpu.SemaphoreType.DMA,
            pltpu.SemaphoreType.DMA((12,)),
            pltpu.SemaphoreType.DMA((12,)),
            pltpu.SemaphoreType.DMA((2,)),
        ],
        compiler_params=pltpu.CompilerParams(
            collective_id=0, has_side_effects=True, vmem_limit_bytes=48 * 1024 * 1024
        ),
        name="sweep",
    )(
        scans.reshape(rows * subjects, trs),
        spatial_init[0],
        time_init,
        subject_init,
        hrf_kernel,
        kept_blocks,
    )
    return updated[None], time_factors, subject_factors


def solution(mesh):
    return jax.shard_map(
        per_device,
        mesh=mesh,
        in_specs=(
            P("mod", "vox", None, "tm"),
            P("mod", "vox", None),
            P("tm", None),
            P(),
            P(),
            P(None, "tm"),
        ),
        out_specs=(P("mod", "vox", None), P("tm", None), P()),
        check_vma=False,
    )
```

time: 1490 us -> 104 us (0.07)
  waiting for transfers between devices: 1200 us -> 0 us
  blocking collectives: 115 us -> 0 us
  other arithmetic: 109 us -> 0 us
  Pallas kernels: 0 us -> 94.8 us
  matrix products: 18.6 us -> 0 us
  local copies, waits for them, and re-layouts: 23.8 us -> 7.68 us
    psum x5 -> x0, waiting for transfers between devices: 1190 us -> none  [the longest x1 429 us: per_device(): row_gram = lax.psum(rgram_part, 'vox')]
    psum x2 -> x0, blocking collectives: 115 us -> none  [the longest x1 107 us: per_device(): subject_rhs, gram_c = lax.psum((subj_part, gram_term), ('vox', 'tm', 'mod'))]
    pallas_call x0 -> x1, Pallas kernels: none -> 94.8 us  [per_device(): pl.pallas_call(functools.partial(sweep, (nz, ntm, nmod)), out_shape=(jax....]
    another operation x15 -> x0, other arithmetic: 70.9 us -> none  [the longest x9 38 us: ridge_solve(): factor = jnp.linalg.cholesky(gram + RIDGE * eye_mat)]
    select_n x4 -> x0, other arithmetic: 32.9 us -> none  [the longest x1 10.8 us: per_device(): adjoint = jnp.where(is_fmri, conv_adjoint(proj, hrf_kernel), proj)]
  transfers between devices with their start and end apart: 8 -> 0, of which waited for: 7 -> 0; matrix products, arithmetic and copies ran while one was open for 2% -> 0% of each run, Pallas kernels for 0% -> 0%
where the time goes in v1:
time: 104 us; the launch traced here: 103 us
  Pallas kernels  94.8 us (91%)
  local copies, waits for them, and re-layouts  7.68 us (7%)
    pallas_call x1, Pallas kernels, per_device(): pl.pallas_call(functools.partial(sweep, (nz, ntm, nmod)), out_shape=(jax....  94.8 us
    unnamed x14, local copies, waits for them, and re-layouts  7.68 us

profile of v1, /device:TPU:1, one launch (start us, length us, event | category | flops | bytes accessed | tf_op | source)
XLA Modules:
  0.0 103.1 jit_solution(179755132239976607)
XLA Ops:
  0.6 0.8 copy.9.kept
  1.4 0.0 copy-start
  1.4 1.9 %copy-done = bf16[1,256,48,128]{3,2,1,0:T(8,128)(2,1)S(1)} copy-done((bf16[1,256,48,128]{3,2,1,0:T(8,128)(2,1)S(1)}, bf16[1,256,48,128]{3,2,1,0:T(8,128)(2,1)}, u32[]{:S(2)}) %copy-start) | copy-done | bytes 3145752
  3.3 0.0 copy-start.1
  3.3 0.9 copy-done.1
  4.2 0.0 copy-start.2
  4.2 0.8 copy-done.2
  5.0 0.0 copy-start.3
  5.0 0.7 copy-done.3
  5.8 0.0 copy-start.4
  5.8 0.7 copy-done.4
  6.4 94.8 %sweep.1 = (f32[256,128]{1,0:T(8,128)S(1)}, f32[128,128]{1,0:T(8,128)S(1)}, f32[48,128]{1,0:T(8,128)S(1)}) custom-call(bf16[12288,128]{1,0:T(8,128)(2,1)S(1)} %bitcast.3, f32[256,128]{1,0:T(8,128)S(1)} %bitcast.4, f32[128,128]{1,0:T(8,128)S(1)} %copy-done.2, f32[48,128]{1,0:T(8,128)S(1)} %copy-done.3, f32[16]{0:T(128)S(1)} %copy-done.4, s32[48,8]{1,0:T(8,128)S(1)} %copy.9.kept), custom_call_target="tpu_custom_call" | custom-call | tf_op jit(solution)/shard_map/sweep/pallas_call | solution.py:451
  101.2 0.7 copy.13
  101.8 0.6 copy.14
  102.5 0.6 copy.15
Async XLA Ops:
  1.4 1.9 %copy-start = (bf16[1,256,48,128]{3,2,1,0:T(8,128)(2,1)S(1)}, bf16[1,256,48,128]{3,2,1,0:T(8,128)(2,1)}, u32[]{:S(2)}) copy-start(bf16[1,256,48,128]{3,2,1,0:T(8,128)(2,1)} %param.6) | copy-start | bytes 9437188
  3.3 0.9 copy-start.1
  4.2 0.8 copy-start.2
  5.0 0.7 copy-start.3
  5.8 0.7 copy-start.4

commit v2 on v1

--- a/solution.py
+++ b/solution.py
@@ -1,4 +1,5 @@
 import functools
+import math
 
 import jax
 import jax.numpy as jnp
@@ -24,50 +25,54 @@
     )
 
 
-def spd_inverse(gram):
+def ridged(gram):
     n = gram.shape[0]
+    at = [lax.broadcasted_iota(jnp.int32, (n, n), d) for d in range(2)]
+    return gram + jnp.where(at[0] == at[1], RIDGE, 0.0)
+
+
+def eliminate(mat):
+    n = mat.shape[0]
     lane = lax.broadcasted_iota(jnp.int32, (8, n), 1)
     sub = lax.broadcasted_iota(jnp.int32, (8, n), 0)
-    eye8 = jnp.where(lane == sub, 1.0, 0.0)
     inside = lane < 8
-    ridge = jnp.where(
-        lax.broadcasted_iota(jnp.int32, (n, n), 0) == lax.broadcasted_iota(jnp.int32, (n, n), 1),
-        RIDGE,
-        0.0,
-    )
-
-    def step(_, mat):
-        top = mat[0:8]
-        cols = [jnp.broadcast_to(top[:, j : j + 1], (8, n)) for j in range(8)]
-        row = jnp.where(inside, eye8, top)
-        for i in range(8):
-            gain = jnp.where(sub == i, -1.0, cols[i]) * (1.0 / cols[i][i : i + 1])
-            row = jnp.where(sub == i, 0.0, row) - gain * row[i : i + 1]
-            for j in range(i + 1, 8):
-                cols[j] = jnp.where(sub == i, 0.0, cols[j]) - gain * cols[j][i : i + 1]
-        rows = []
-        for b in range(1, n // 8):
-            below = mat[8 * b : 8 * b + 8]
-            left = jnp.where(inside, 0.0, below)
-            for j in range(8):
-                left = left - jnp.broadcast_to(below[:, j : j + 1], (8, n)) * row[j : j + 1]
-            rows.append(left)
-        return pltpu.roll(jnp.concatenate(rows + [row]), n - 8, 1)
-
-    return lax.fori_loop(0, n // 8, step, gram + ridge, unroll=2)
+    top = mat[0:8]
+    cols = [jnp.broadcast_to(top[:, j : j + 1], (8, n)) for j in range(8)]
+    row = jnp.where(inside, jnp.where(lane == sub, 1.0, 0.0), top)
+    for i in range(8):
+        gain = jnp.where(sub == i, -1.0, cols[i]) * (1.0 / cols[i][i : i + 1])
+        row = jnp.where(sub == i, 0.0, row) - gain * row[i : i + 1]
+        for j in range(i + 1, 8):
+            cols[j] = jnp.where(sub == i, 0.0, cols[j]) - gain * cols[j][i : i + 1]
+    rows = []
+    for b in range(1, n // 8):
+        below = mat[8 * b : 8 * b + 8]
+        left = jnp.where(inside, 0.0, below)
+        for j in range(8):
+            left = left - jnp.broadcast_to(below[:, j : j + 1], (8, n)) * row[j : j + 1]
+        rows.append(left)
+    return pltpu.roll(jnp.concatenate(rows + [row]), n - 8, 1)
+
+
+def eliminations(count, mat):
+    return lax.fori_loop(0, count, lambda _, m: eliminate(m), mat, unroll=2)
 
 
 def sweep(
     sizes,
     scans,
-    spatial,
+    spatial_in,
     time_init,
-    subject,
+    subject_in,
     hrf,
-    kept,
+    kept_in,
     out_spatial,
     out_time,
     out_subject,
+    spatial,
+    subject,
+    kept,
+    win,
     x_in,
     x_f32,
     xs,
@@ -93,7 +98,6 @@
     s1,
     s2,
     s_sum,
-    s_own,
     s_all,
     local_sem,
     send_sem,
@@ -115,15 +119,19 @@
     rplace = c4 * nmod + mod
     grow = rank // ngram
     rrow = trs // nrhs
-    srow = subjects // nz
+    srow = -(-subjects // nplane)
     own = pl.ds(pl.multiple_of(trs * tm, trs), trs)
     part = rows // ntm
     my_part = pl.ds(pl.multiple_of(part * tm, part), part)
 
+    def far(i):
+        return nz // 2 + (1 - 2 * lax.rem(i, 2)) * (i // 2)
+
     def along_tm(d):
         return (vox, lax.rem(tm + d, ntm), mod)
 
-    def along_z(d):
+    def along_z(i):
+        d = far(i)
         return (lax.rem(z + d, nz) * PLANE + c4, tm, mod)
 
     def in_plane(d):
@@ -150,8 +158,6 @@
     def wait(sem, stage, ref):
         pltpu.make_async_copy(ref, ref, sem.at[stage]).wait()
 
-    load = pltpu.make_async_copy(scans, x_in, local_sem)
-    load.start()
     barrier = pltpu.get_barrier_semaphore()
     every(
         nplane,
@@ -160,13 +166,28 @@
     every(
         nz, lambda d: pl.semaphore_signal(barrier, 1, device_id=along_z(d), device_id_type=MESH)
     )
+    own_pad = pl.ds(pl.multiple_of(reach + trs * tm, 8), trs)
+    loads = [
+        pltpu.make_async_copy(src, dst, local_sem.at[i])
+        for i, (src, dst) in enumerate(
+            (
+                (scans, x_in),
+                (subject_in, subject),
+                (kept_in, kept),
+                (spatial_in, spatial),
+                (time_init, pad.at[own_pad]),
+            )
+        )
+    ]
+    for load in loads:
+        load.start()
     pl.semaphore_wait(barrier, nplane + nz - 2)
 
     pad[0:reach] = jnp.zeros((reach, rank), jnp.float32)
-    own_pad = pl.ds(pl.multiple_of(reach + trs * tm, 8), trs)
     every(ntm, lambda d: send(0, time_init, pad.at[own_pad], along_tm(d)))
 
-    load.wait()
+    for load in loads:
+        load.wait()
 
     def widen(i, carry):
         at = pl.ds(pl.multiple_of(i * 512, 512), 512)
@@ -182,13 +203,10 @@
         return carry
 
     lax.fori_loop(0, subjects, regroup, 0)
-    block = trs // kept.shape[1]
-    block_of = lax.broadcasted_iota(jnp.int32, (subjects, trs), 1) // block
-    flags = kept[...]
-    keep = jnp.zeros((subjects, trs), jnp.int32)
-    for b in range(kept.shape[1]):
-        keep = jnp.where(block_of == b, flags[:, b : b + 1], keep)
-    mask[...] = jnp.where(mod == 0, keep, 1).astype(jnp.float32)
+    block = trs // kept.shape[0]
+    spot = [lax.broadcasted_iota(jnp.int32, (kept.shape[0], trs), d) for d in range(2)]
+    spans = jnp.where(spot[1] // block == spot[0], 1.0, 0.0)
+    mask[...] = jnp.where(mod == 0, tdot(kept[...].astype(jnp.float32), spans), 1.0)
     subj = subject[...]
     subj_gram = tdot(subj, subj)
     previous = spatial[...].astype(jnp.bfloat16)
@@ -196,7 +214,6 @@
     lags = [hrf[k] for k in range(reach)]
     taps = [jnp.where(is_fmri, lags[k], 1.0 if k == 0 else 0.0) for k in range(reach)]
 
-    pad[own_pad] = time_init[...]
     wait(recv_sem, 0, pad.at[pl.ds(reach, (ntm - 1) * trs)])
 
     def conv(weights, base):
@@ -213,8 +230,7 @@
 
     rhs[...] = jnp.zeros_like(rhs)
 
-    def fill(i, carry):
-        s = 2 * i
+    def fill_pair(s):
         first = pl.ds(pl.multiple_of(s * rows, rows), rows)
         second = pl.ds(pl.multiple_of((s + 1) * rows, rows), rows)
         khatri = jnp.concatenate(
@@ -237,16 +253,24 @@
         rhs[...] += jnp.dot(
             jnp.concatenate([f0, f1], axis=1), khatri, preferred_element_type=jnp.float32
         )
-        return carry
-
-    lax.fori_loop(0, subjects // 2, fill, 0)
+
+    steps = rank // 8
+    turns = math.gcd(subjects // 2, steps)
+
+    def fill(i, mat):
+        for j in range(subjects // 2 // turns):
+            fill_pair(2 * (i * (subjects // 2 // turns) + j))
+        for j in range(steps // turns):
+            mat = eliminate(mat)
+        return mat
+
+    inverse = lax.fori_loop(0, turns, fill, ridged(subj_gram * time_gram))
 
     def scatter_rows(d):
         to = pl.multiple_of(part * lax.rem(tm + d, ntm), part)
         send(1, rhs.at[pl.ds(to, part)], rhs_in.at[d - 1], along_tm(d))
 
     every(ntm, scatter_rows)
-    inverse = spd_inverse(subj_gram * time_gram)
     wait(recv_sem, 1, rhs_in)
     mine = rhs[my_part]
     for d in range(ntm - 1):
@@ -291,7 +315,9 @@
             filled, khatri, (((0,), (0,)), ((), ())), preferred_element_type=jnp.float32
         )
 
-    proj = lax.fori_loop(0, subjects // 2, project, jnp.zeros((trs, rank), jnp.float32))
+    proj = lax.fori_loop(
+        0, subjects // 2, project, jnp.zeros((trs, rank), jnp.float32), unroll=8
+    )
     ppad[0:reach] = jnp.zeros((reach, rank), jnp.float32)
     ppad[reach : reach + trs] = proj
     ppad[reach + trs :] = jnp.zeros((reach, rank), jnp.float32)
@@ -355,7 +381,7 @@
     grams = [
         jnp.concatenate([g_all[m * ngram + i] for i in range(ngram)]) for m in range(nmod)
     ]
-    inverse = spd_inverse((grams[0] + grams[1]) * subj_gram)
+    inverse = eliminations(steps // 2, ridged((grams[0] + grams[1]) * subj_gram))
 
     wait(recv_sem, 7, r2.at[pl.ds(0, nz - 1)])
     mine = r2[0]
@@ -365,18 +391,18 @@
     r_own = tm * nrhs + rplace
     r_all[r_own] = mine
     every(nplane, lambda d: send(8, r_sum, r_all.at[r_own], in_plane(d)))
+    inverse = eliminations(steps - steps // 2, inverse)
     wait(recv_sem, 8, r_all.at[pl.ds(0, nplane - 1)])
     right = jnp.concatenate([r_all[i] for i in range(ntm * nrhs)])
     raw = (rows * nz * PLANE) * dot(right, inverse)
     mean = jnp.sum(raw * raw, axis=0, keepdims=True) / (ntm * trs)
     fresh = raw / jnp.sqrt(mean + EPS)
     scale_c = (2.0 * rows * nz * PLANE * trs * ntm) ** (-0.5)
-    pad[reach:] = fresh
-    out_time[...] = pad[own_pad]
     pad[reach:] = fresh * scale_c
-    for i in range(ntm):
-        factors[i * trs : (i + 1) * trs] = conv(lags, i * trs)
-    scaled = jnp.where(is_fmri, factors[own], pad[own_pad])
+    win[...] = pad[pl.ds(pl.multiple_of(trs * tm, trs), reach + trs)]
+    scaled = taps[0] * win[reach:]
+    for k in range(1, reach):
+        scaled = scaled + taps[k] * win[reach - k : reach - k + trs]
     high = scaled.astype(jnp.bfloat16)
     low = (scaled - high.astype(jnp.float32)).astype(jnp.bfloat16)
     halves = jnp.concatenate([high, low], axis=1)
@@ -396,29 +422,39 @@
         s_part[i] = jnp.concatenate(lines)
         return carry
 
-    lax.fori_loop(0, nz, contract, 0)
-    every(nz, lambda d: send(9, s_part.at[lax.rem(z + d, nz)], s1.at[d - 1], along_z(d)))
+    lax.fori_loop(0, subjects // srow, contract, 0, unroll=6)
+    for i in range(subjects // srow, nplane):
+        s_part[i] = jnp.zeros((srow, rank), jnp.float32)
+    every(
+        nplane,
+        lambda d: send(9, s_part.at[lax.rem(place + d, nplane)], s1.at[d - 1], in_plane(d)),
+    )
+    for i in range(ntm):
+        factors[i * trs : (i + 1) * trs] = conv(lags, i * trs)
     eeg = pad[reach:]
     fmri = factors[...]
+    pad[reach:] = fresh
+    out_time[...] = pad[own_pad]
     gram_c = grams[0] * tdot(fmri, fmri) + grams[1] * tdot(eeg, eeg)
 
     wait(recv_sem, 9, s1)
-    mine = s_part[z]
-    for d in range(nz - 1):
+    mine = s_part[place]
+    for d in range(nplane - 1):
         mine = mine + s1[d]
-    s_own[...] = mine
-    s2[place] = mine
-    every(nplane, lambda d: send(10, s_own, s2.at[place], in_plane(d)))
-    inverse = spd_inverse(gram_c)
-    wait(recv_sem, 10, s2.at[pl.ds(0, nplane - 1)])
+    s2[z] = mine
+    every(nz, lambda d: send(10, s2.at[z], s2.at[z], along_z(d)))
+    inverse = eliminations(steps, ridged(gram_c))
+    wait(recv_sem, 10, s2.at[pl.ds(0, nz - 1)])
     mine = s2[0]
-    for i in range(1, nplane):
+    for i in range(1, nz):
         mine = mine + s2[i]
     s_sum[...] = mine
-    s_all[z] = mine
-    every(nz, lambda d: send(11, s_sum, s_all.at[z], along_z(d)))
-    wait(recv_sem, 11, s_all.at[pl.ds(0, nz - 1)])
-    out_subject[...] = dot(jnp.concatenate([s_all[i] for i in range(nz)]), inverse)
+    s_all[place] = mine
+    every(nplane, lambda d: send(11, s_sum, s_all.at[place], in_plane(d)))
+    wait(recv_sem, 11, s_all.at[pl.ds(0, nplane - 1)])
+    out_subject[...] = dot(
+        jnp.concatenate([s_all[i] for i in range(subjects // srow)]), inverse
+    )
 
     wait(send_sem, 0, pad.at[pl.ds(reach, (ntm - 1) * trs)])
     wait(send_sem, 1, rhs_in)
@@ -430,8 +466,8 @@
     wait(send_sem, 7, r2.at[pl.ds(0, nz - 1)])
     wait(send_sem, 8, r_all.at[pl.ds(0, nplane - 1)])
     wait(send_sem, 9, s1)
-    wait(send_sem, 10, s2.at[pl.ds(0, nplane - 1)])
-    wait(send_sem, 11, s_all.at[pl.ds(0, nz - 1)])
+    wait(send_sem, 10, s2.at[pl.ds(0, nz - 1)])
+    wait(send_sem, 11, s_all.at[pl.ds(0, nplane - 1)])
 
     @pl.when(gives_halo)
     def _():
@@ -445,9 +481,9 @@
     rank = subject_init.shape[1]
     reach = hrf_kernel.shape[0]
     nplane, ngram, nrhs = PLANE * ntm * nmod, PLANE * ntm, PLANE * nmod
-    grow, rrow, srow = rank // ngram, trs // nrhs, subjects // nz
+    grow, rrow, srow = rank // ngram, trs // nrhs, -(-subjects // nplane)
     f32, bf16 = jnp.float32, jnp.bfloat16
-    vmem = pl.BlockSpec(memory_space=pltpu.VMEM)
+    anywhere = pl.BlockSpec(memory_space=pl.ANY)
     updated, time_factors, subject_factors = pl.pallas_call(
         functools.partial(sweep, (nz, ntm, nmod)),
         out_shape=(
@@ -455,16 +491,13 @@
             jax.ShapeDtypeStruct((trs, rank), f32),
             jax.ShapeDtypeStruct((subjects, rank), f32),
         ),
-        in_specs=[
-            pl.BlockSpec(memory_space=pl.ANY),
-            vmem,
-            vmem,
-            vmem,
-            pl.BlockSpec(memory_space=pltpu.SMEM),
-            vmem,
-        ],
-        out_specs=(vmem, vmem, vmem),
+        in_specs=[anywhere] * 4 + [pl.BlockSpec(memory_space=pltpu.SMEM), anywhere],
+        out_specs=(pl.BlockSpec(memory_space=pltpu.VMEM),) * 3,
         scratch_shapes=[
+            pltpu.VMEM((rows, rank), f32),
+            pltpu.VMEM((subjects, rank), f32),
+            pltpu.VMEM(kept_blocks.shape[::-1], jnp.int32),
+            pltpu.VMEM((reach + trs, rank), f32),
             pltpu.VMEM((rows * subjects, trs), bf16),
             pltpu.VMEM((rows * subjects, trs), f32),
             pltpu.VMEM((subjects * rows, trs), bf16),
@@ -486,19 +519,18 @@
             pltpu.VMEM((nz, rrow, rank), f32),
             pltpu.VMEM((rrow, rank), f32),
             pltpu.VMEM((nplane, rrow, rank), f32),
+            pltpu.VMEM((nplane, srow, rank), f32),
+            pltpu.VMEM((nplane - 1, srow, rank), f32),
             pltpu.VMEM((nz, srow, rank), f32),
-            pltpu.VMEM((nz - 1, srow, rank), f32),
+            pltpu.VMEM((srow, rank), f32),
             pltpu.VMEM((nplane, srow, rank), f32),
-            pltpu.VMEM((srow, rank), f32),
-            pltpu.VMEM((srow, rank), f32),
-            pltpu.VMEM((nz, srow, rank), f32),
-            pltpu.SemaphoreType.DMA,
+            pltpu.SemaphoreType.DMA((5,)),
             pltpu.SemaphoreType.DMA((12,)),
             pltpu.SemaphoreType.DMA((12,)),
             pltpu.SemaphoreType.DMA((2,)),
         ],
         compiler_params=pltpu.CompilerParams(
-            collective_id=0, has_side_effects=True, vmem_limit_bytes=48 * 1024 * 1024
+            collective_id=0, has_side_effects=True, vmem_limit_bytes=62 * 1024 * 1024
         ),
         name="sweep",
     )(
@@ -507,7 +539,7 @@
         time_init,
         subject_init,
         hrf_kernel,
-        kept_blocks,
+        kept_blocks.T,
     )
     return updated[None], time_factors, subject_factors
 

time: 104 us -> 88.3 us (0.85)
  Pallas kernels: 94.8 us -> 83.1 us
  local copies, waits for them, and re-layouts: 7.68 us -> 4.39 us
    pallas_call x1, Pallas kernels: 94.8 us -> 83.1 us  [per_device(): pl.pallas_call(functools.partial(sweep, (nz, ntm, nmod)), out_shape=(jax....]
    unnamed x14 -> x3, local copies, waits for them, and re-layouts: 7.68 us -> 4.39 us
where the time goes in v2:
time: 88.3 us; the launch traced here: 88.1 us
  Pallas kernels  83.1 us (94%)
  local copies, waits for them, and re-layouts  4.39 us (5%)
    pallas_call x1, Pallas kernels, per_device(): pl.pallas_call(functools.partial(sweep, (nz, ntm, nmod)), out_shape=(jax....  83.1 us
    unnamed x3, local copies, waits for them, and re-layouts  4.39 us

profile of v2, /device:TPU:1, one launch (start us, length us, event | category | flops | bytes accessed | tf_op | source)
XLA Modules:
  0.0 88.1 jit_solution(10991498832079506910)
XLA Ops:
  0.6 83.1 %sweep.1 = (f32[256,128]{1,0:T(8,128)}, f32[128,128]{1,0:T(8,128)}, f32[48,128]{1,0:T(8,128)}) custom-call(bf16[12288,128]{1,0:T(8,128)(2,1)} %bitcast.4, f32[256,128]{1,0:T(8,128)} %bitcast.5, f32[128,128]{1,0:T(8,128)} %time_init.1, f32[48,128]{1,0:T(8,128)} %subject_in.1, f32[16]{0:T(128)} %hrf.1, s32[8,48]{1,0:T(8,128)} %bitcast.7), custom_call_target="tpu_custom_call" | custom-call | tf_op jit(solution)/shard_map/sweep/pallas_call | solution.py:487
  83.7 1.6 %copy.12 = f32[1,256,128]{2,1,0:T(8,128)} copy(f32[1,256,128]{2,1,0:T(8,128)} %bitcast.6) | data formatting | bytes 262144
  85.3 1.5 %copy.13 = f32[128,128]{1,0:T(8,128)} copy(f32[128,128]{1,0:T(8,128)} %get-tuple-element.13) | data formatting | bytes 131072
  86.7 1.3 %copy.14 = f32[48,128]{1,0:T(8,128)} copy(f32[48,128]{1,0:T(8,128)} %get-tuple-element.14) | data formatting | bytes 49152

commit v3 on v2

--- a/solution.py
+++ b/solution.py
@@ -255,12 +255,12 @@
         )
 
     steps = rank // 8
-    turns = math.gcd(subjects // 2, steps)
+    turns = math.gcd(subjects // 2, steps // 2)
 
     def fill(i, mat):
         for j in range(subjects // 2 // turns):
             fill_pair(2 * (i * (subjects // 2 // turns) + j))
-        for j in range(steps // turns):
+        for j in range(steps // 2 // turns):
             mat = eliminate(mat)
         return mat
 
@@ -271,6 +271,7 @@
         send(1, rhs.at[pl.ds(to, part)], rhs_in.at[d - 1], along_tm(d))
 
     every(ntm, scatter_rows)
+    inverse = eliminations(steps - steps // 2, inverse)
     wait(recv_sem, 1, rhs_in)
     mine = rhs[my_part]
     for d in range(ntm - 1):
@@ -381,7 +382,7 @@
     grams = [
         jnp.concatenate([g_all[m * ngram + i] for i in range(ngram)]) for m in range(nmod)
     ]
-    inverse = eliminations(steps // 2, ridged((grams[0] + grams[1]) * subj_gram))
+    inverse = eliminations(steps // 8, ridged((grams[0] + grams[1]) * subj_gram))
 
     wait(recv_sem, 7, r2.at[pl.ds(0, nz - 1)])
     mine = r2[0]
@@ -391,7 +392,7 @@
     r_own = tm * nrhs + rplace
     r_all[r_own] = mine
     every(nplane, lambda d: send(8, r_sum, r_all.at[r_own], in_plane(d)))
-    inverse = eliminations(steps - steps // 2, inverse)
+    inverse = eliminations(steps - steps // 8, inverse)
     wait(recv_sem, 8, r_all.at[pl.ds(0, nplane - 1)])
     right = jnp.concatenate([r_all[i] for i in range(ntm * nrhs)])
     raw = (rows * nz * PLANE) * dot(right, inverse)

time: 88.3 us -> 87 us (0.985)
  Pallas kernels: 83.1 us -> 81.7 us
    pallas_call x1, Pallas kernels: 83.1 us -> 81.7 us  [per_device(): pl.pallas_call(functools.partial(sweep, (nz, ntm, nmod)), out_shape=(jax....]
where the time goes in v3:
time: 87 us; the launch traced here: 86.7 us
  Pallas kernels  81.7 us (94%)
  local copies, waits for them, and re-layouts  4.39 us (5%)
    pallas_call x1, Pallas kernels, per_device(): pl.pallas_call(functools.partial(sweep, (nz, ntm, nmod)), out_shape=(jax....  81.7 us
    unnamed x3, local copies, waits for them, and re-layouts  4.39 us

profile of v3, /device:TPU:1, one launch (start us, length us, event | category | flops | bytes accessed | tf_op | source)
XLA Modules:
  0.0 86.7 jit_solution(789583009983674840)
XLA Ops:
  0.6 81.7 %sweep.1 = (f32[256,128]{1,0:T(8,128)}, f32[128,128]{1,0:T(8,128)}, f32[48,128]{1,0:T(8,128)}) custom-call(bf16[12288,128]{1,0:T(8,128)(2,1)} %bitcast.4, f32[256,128]{1,0:T(8,128)} %bitcast.5, f32[128,128]{1,0:T(8,128)} %time_init.1, f32[48,128]{1,0:T(8,128)} %subject_in.1, f32[16]{0:T(128)} %hrf.1, s32[8,48]{1,0:T(8,128)} %bitcast.7), custom_call_target="tpu_custom_call" | custom-call | tf_op jit(solution)/shard_map/sweep/pallas_call | solution.py:488
  82.4 1.6 %copy.12 = f32[1,256,128]{2,1,0:T(8,128)} copy(f32[1,256,128]{2,1,0:T(8,128)} %bitcast.6) | data formatting | bytes 262144
  83.9 1.5 %copy.13 = f32[128,128]{1,0:T(8,128)} copy(f32[128,128]{1,0:T(8,128)} %get-tuple-element.13) | data formatting | bytes 131072
  85.4 1.3 %copy.14 = f32[48,128]{1,0:T(8,128)} copy(f32[48,128]{1,0:T(8,128)} %get-tuple-element.14) | data formatting | bytes 49152
